TPU v7x, 256 devices: a whole 4x4x8 slice. The times are simulated.
256 devices in a mesh: row: 8 (over x, y_hi), col: 32 (over z, y_lo, core).
Axes of the slice: x: 4, y: 4 (y_hi: 2, y_lo: 2; y = y_hi * 2 + y_lo), z: 8, core: 2. Of those that a mesh axis runs over, the one named last changes fastest.
Arguments:
- density: bfloat16 [8192, 8192], P('row', 'col'), as said below
- pattern: int32 [64, 64], replicated, may hold values from 0 to 1, as said below
Outputs:
- square: bfloat16 [8192, 8192], P('row', 'col')
- traces: float32 [2], replicated
Inputs may be any that keep to these rules, and one draw needn't show every extreme that they name: Every diagonal block of 128 x 128 entries of density is symmetric. `pattern`: block (0, 63) is always stored.
All inputs are finite; a program needn't handle non-finite values.
Results may differ from a plain program's by a relative error of at most 0.0013.
Values may be sent and summed in bfloat16 or wider, within the bound.
A program may use at most 64 MiB of HBM per device.

v0:
```python
import jax
import jax.numpy as jnp
from jax import lax
from jax.sharding import PartitionSpec as P

BLK = 128


def spread(value, axis, source):
    kept = jnp.where(lax.axis_index(axis) == source, value, 0).astype(value.dtype)
    return lax.psum(kept, axis)


def block_masks(row_start, row_count, col_start, col_count, pattern):
    block_rows = row_start + jnp.arange(row_count)
    block_cols = col_start + jnp.arange(col_count)
    chosen = lax.dynamic_slice(
        pattern, (jnp.asarray(row_start), jnp.asarray(col_start)), (row_count, col_count)
    )
    diagonal_blk = block_rows[:, None] == block_cols[None, :]
    above = block_cols[None, :] >= block_rows[:, None]
    kept_blocks = ((chosen != 0) | diagonal_blk) & above
    strict_blocks = kept_blocks & jnp.logical_not(diagonal_blk)
    return (kept_blocks, strict_blocks)


def masked(values, block_mask):
    row_count, col_count = block_mask.shape
    shaped = values.reshape(row_count, BLK, col_count, BLK)
    kept = jnp.where(block_mask[:, None, :, None], shaped, jnp.zeros_like(shaped))
    return kept.reshape(values.shape)


def complete_panel(column, panel_rows, col_index, pattern):
    panel_width = column.shape[1]
    order_size = column.shape[0]
    col_blocks = panel_width // BLK
    panel_rows = panel_rows.reshape(panel_width, order_size)
    mirror_kept, mirror_strict = block_masks(
        col_index * col_blocks, col_blocks, jnp.int32(0), order_size // BLK, pattern
    )
    mirrored = masked(panel_rows, mirror_strict)
    full_column = column + mirrored.T
    return full_column


def per_device(density, pattern):
    n_row = lax.axis_size("row")
    n_col = lax.axis_size("col")
    sub_count = n_col // n_row
    row_index = lax.axis_index("row")
    col_index = lax.axis_index("col")
    panel_height, panel_width = density.shape
    order_size = panel_width * n_col
    row_blocks = panel_height // BLK
    col_blocks = panel_width // BLK
    kept_blocks, strict_blocks = block_masks(
        row_index * row_blocks, row_blocks, col_index * col_blocks, col_blocks, pattern
    )
    stored = masked(density, kept_blocks)
    column = lax.all_gather(stored, "row", axis=0, tiled=True)
    pieces = stored.reshape(sub_count, panel_width, panel_width)
    outgoing = jnp.tile(pieces, (n_col // sub_count, 1, 1))
    own_upper = lax.all_to_all(outgoing, "col", split_axis=0, concat_axis=2, tiled=True)
    panel_rows = spread(own_upper, "row", col_index // sub_count)
    full_column = complete_panel(column, panel_rows, col_index, pattern)
    own_rows = lax.dynamic_slice_in_dim(full_column, row_index * panel_height, panel_height, 0)
    global_rows = row_index * panel_height + jnp.arange(panel_height)[:, None]
    global_cols = col_index * panel_width + jnp.arange(panel_width)[None, :]
    on_diag = global_rows == global_cols
    trace_local = jnp.sum(jnp.where(on_diag, stored, jnp.zeros_like(stored)).astype(jnp.float32))
    product = jnp.dot(
        lax.all_gather(own_rows, "col", axis=1, tiled=True),
        full_column,
        preferred_element_type=jnp.float32,
    )
    trace_square = jnp.sum(jnp.where(on_diag, product, jnp.zeros_like(product)))
    trace_sums = lax.psum((trace_local, trace_square), ("row", "col"))
    square = masked(product, kept_blocks).astype(jnp.bfloat16)
    traces = jnp.stack([trace_sums[0], trace_sums[1]]) / order_size
    return (square, traces)


def solution(mesh):
    placed = (P("row", "col"), P())
    return jax.shard_map(
        per_device, mesh=mesh, in_specs=placed, out_specs=(P("row", "col"), P()), check_vma=False
    )
```

profile of v0, /device:TPU:88, one launch (start us, length us, event | category | flops | bytes accessed | tf_op | source)
XLA Modules:
  0.0 546.7 jit_solution(13792541607843465299)
XLA Ops:
  7.2 0.8 fusion.2
  8.0 0.1 copy.6
  8.1 0.1 broadcast_in_dim.58
  8.2 0.4 broadcast_in_dim.63
  8.6 1.3 copy.12
  9.9 0.4 broadcast_select_fusion.1
  10.3 0.1 copy.9
  10.4 2.4 tile.8
  12.9 9.4 %all-to-all-start = ((bf16[32,256,256]{1,2,0:T(8,128)(2,1)}), bf16[32,256,256]{1,2,0:T(8,128)(2,1)}, u32[]{:S(2)}, u32[]{:S(2)}) async-start(bf16[32,256,256]{1,2,0:T(8,128)(2,1)} %bitcast.29), calls=%async_computation | async-start | bytes 8388608 | tf_op jit(solution)/shard_map/all_to_all | solution.py:64
  22.2 0.0 all-gather.3.cloned.1.call-start
  22.3 0.1 copy.18
  22.4 0.3 copy.11
  22.8 0.9 broadcast_select_fusion.2
  23.7 0.0 all-gather.3.cloned.1.call-update
  23.7 0.0 all-reduce.3.cloned.1.call-start
  23.8 93.1 %all-to-all-done = bf16[32,256,256]{1,2,0:T(8,128)(2,1)} async-done(((bf16[32,256,256]{1,2,0:T(8,128)(2,1)}), bf16[32,256,256]{1,2,0:T(8,128)(2,1)}, u32[]{:S(2)}, u32[]{:S(2)}) %all-to-all-start) | async-done | bytes 4194336 | tf_op jit(solution)/shard_map/all_to_all | solution.py:64
  116.9 2.2 broadcast_select_fusion
  119.2 0.0 all-gather.5.cloned.1.call-start
  119.2 0.8 not_and_fusion
  120.0 0.6 broadcast_in_dim.61
  120.6 3.5 copy.17
  124.1 5.9 %copy.10 = pred[256,8192]{0,1:T(8,128)(4,1)S(1)} copy(pred[256,8192]{1,0:T(8,128)(4,1)} %bitcast.32) | data formatting | bytes 4194304 | tf_op jit(solution)/shard_map/jit(_where)/broadcast_in_dim | solution.py:30
  130.0 0.0 all-gather.3.cloned.1.call-done
  130.0 187.9 %all-reduce.3.cloned.1.call-done = bf16[256,8192]{0,1:T(8,128)(2,1)} async-done(((bf16[256,8192]{0,1:T(8,128)(2,1)}), bf16[256,8192]{0,1:T(8,128)(2,1)}) %all-reduce.3.cloned.1.call-update) | async-done | bytes 4194320 | tf_op jit(solution)/shard_map/psum | solution.py:11
  317.9 4.0 bitcast_add_fusion
  321.9 1.9 copy-done
  323.8 0.8 constant_dynamic-slice_fusion
  324.7 127.1 %all-gather.5.cloned.1.call-done = bf16[1024,8192]{1,0:T(8,128)(2,1)} async-done(((bf16[1024,256]{1,0:T(8,128)(2,1)}), bf16[1024,8192]{1,0:T(8,128)(2,1)}) %all-gather.5.cloned.1.call-update) | async-done | bytes 16777232 | tf_op jit(solution)/shard_map/all_gather | solution.py:73
  451.8 12.2 %select_convert_fusion = (bf16[1024,256]{1,0:T(8,128)(2,1)}, f32[1024,256]{1,0:T(8,128)S(1)}) fusion(pred[1024,256]{1,0:T(32,128)(4,1)S(1)} %copy.11, bf16[1024,8192]{1,0:T(8,128)(2,1)} %all-gather.5.cloned.1.call-done, bf16[8192,256]{1,0:T(8,128)(2,1)} %copy-done), kind=kOutput, calls=%fused_computation.7 | convolution fusion | flops 4295229440 | bytes 22806528 | tf_op jit(solution)/shard_map/dot_general | solution.py:72
  464.1 1.0 convert_reduce_fusion
  465.1 73.3 %all-reduce = (f32[1]{0:T(128)}, f32[1]{0:T(128)}) all-reduce(f32[1]{0:T(128)} %bitcast.7, f32[1]{0:T(128)} %bitcast.6), channel_id=1, replica_groups=mesh['row'=8,'col'=32] {'row','col'}, use_global_device_ids=true, to_apply=%region_4.5 | all-reduce | flops 2 | bytes 16 | tf_op jit(solution)/shard_map/psum | solution.py:78
  538.4 1.8 maximum_multiply_fusion
  (11 shorter events, 0.1 us)
Async XLA Ops:
  12.9 9.9 %copy-start.2 = (bf16[1024,256]{1,0:T(8,128)(2,1)S(1)}, bf16[1024,256]{1,0:T(8,128)(2,1)}, u32[]{:S(2)}) copy-start(bf16[1024,256]{1,0:T(8,128)(2,1)} %param.2) | copy-start | bytes 1572868
  12.9 104.1 %all-to-all-start = ((bf16[32,256,256]{1,2,0:T(8,128)(2,1)}), bf16[32,256,256]{1,2,0:T(8,128)(2,1)}, u32[]{:S(2)}, u32[]{:S(2)}) async-start(bf16[32,256,256]{1,2,0:T(8,128)(2,1)} %bitcast.29), calls=%async_computation | async-start | bytes 8388608 | tf_op jit(solution)/shard_map/all_to_all | solution.py:64
  22.2 107.8 %all-gather.3.cloned.1.call-start = ((), (), s32[]{:S(2)}) async-start(), calls=%async_computation.1 | async-start | bytes 4718592 | tf_op jit(solution)/shard_map/all_gather | solution.py:61
  23.7 294.2 %all-reduce.3.cloned.1.call-start = ((), (), s32[]{:S(2)}) async-start(), calls=%async_computation.2 | async-start | bytes 8388608 | tf_op jit(solution)/shard_map/psum | solution.py:11
  119.2 332.6 %all-gather.5.cloned.1.call-start = ((), (), s32[]{:S(2)}) async-start(), calls=%async_computation.3 | async-start | bytes 17301504 | tf_op jit(solution)/shard_map/all_gather | solution.py:73
  321.9 1.9 copy-start
  324.7 139.4 %copy-start.1 = (bf16[1024,256]{1,0:T(8,128)(2,1)S(1)}, bf16[1024,256]{1,0:T(8,128)(2,1)}, u32[]{:S(2)}) copy-start(bf16[1024,256]{1,0:T(8,128)(2,1)} %broadcast_select_fusion.2) | copy-start | bytes 1572868
Sparse Core Ops, SparseCore 0:
  25.7 101.3 all-gather.2
  129.7 188.1 all-reduce.2
  324.8 126.9 all-gather.4
where the time goes:
time: 553 us; the launch traced here: 547 us
  waiting for transfers between devices  408 us (74%)
  blocking collectives  73.3 us (13%)
  local copies, waits for them, and re-layouts  17.7 us (3%)
  between operations  13.9 us (3%)
  matrix products  12.2 us (2%)
  other arithmetic  12 us (2%)
  starting transfers between devices  9.49 us (2%)
    psum x1, waiting for transfers between devices, spread(): return lax.psum(kept, axis)  188 us
    all_gather x1, waiting for transfers between devices, per_device(): lax.all_gather(own_rows, 'col', axis=1, tiled=True)  127 us
    all_to_all x1, waiting for transfers between devices, per_device(): lax.all_to_all(outgoing, 'col', split_axis=0, concat_axis=2, tiled=True)  93.1 us
    psum x1, blocking collectives, per_device(): trace_sums = lax.psum((trace_local, trace_square), ('row', 'col'))  73.3 us
    dot_general x1, matrix products, per_device(): jnp.dot(lax.all_gather(own_rows, 'col', axis=1, tiled=True), full_column,...  12.2 us
  transfers between devices with their start and end apart: 4, of which 3 were waited for; matrix products, arithmetic and copies ran while one was open for 3% of the time, Pallas kernels for 0%

commit v1 on v0

v1 whole, which is shorter than its diff:
```python
import jax
import jax.numpy as jnp
from jax import lax
from jax.experimental import pallas as pl
from jax.experimental.pallas import tpu as pltpu
from jax.sharding import PartitionSpec as P

BLK = 128
MESH = pl.DeviceIdType.MESH
TILE = 256
SUPER = 1024
NSUP = 8
CHUNKS = 4


def ring_order(r, p):
    x, hi = lax.div(r, 2), lax.rem(r, 2)
    xx = lax.rem(x + 2 * p, 4)
    return xx * (1 - hi) + (7 - xx) * hi


def ring_row(h, p):
    hi = lax.div(h, 4)
    xx = h * (1 - hi) + (7 - h) * hi
    return 2 * lax.rem(xx + 2 * p, 4) + hi


def kernel(
    pat, dens, out,
    tbuf, ttbuf, rowb, colb, part, sibb, ysend, yrecv,
    ring_s, ring_r, intra_s, intra_r, mirr_s, mirr_r, mirc_s, mirc_r,
    sib_s, sib_r, y_s, y_r,
):
    r = lax.axis_index("row")
    c = lax.axis_index("col")
    z, s = lax.div(c, 4), lax.rem(c, 4)
    p, q = lax.div(s, 2), lax.rem(s, 2)
    upper, diag, lower = r < z, r == z, r > z

    def dev(r_, z_, s_):
        return (r_, 4 * z_ + s_)

    def copy(src, dst, ssem, rsem, device):
        return pltpu.make_async_remote_copy(
            src_ref=src, dst_ref=dst, send_sem=ssem, recv_sem=rsem,
            device_id=device, device_id_type=MESH,
        )

    h = ring_order(r, p)
    z_next, z_prev = lax.rem(z + 1, 8), lax.rem(z + 7, 8)
    r_next, r_prev = ring_row(lax.rem(h + 1, 8), p), ring_row(lax.rem(h + 7, 8), p)
    neighbours = (
        (dev(r, z_next, s), dev(r, z_prev, s)),
        (dev(r_next, z, s), dev(r_prev, z, s)),
    )
    others = [lax.rem(s + d, 4) for d in (1, 2, 3)]

    barrier = pltpu.get_barrier_semaphore()
    for ring in neighbours:
        for device in ring:
            pl.semaphore_signal(barrier, inc=1, device_id=device, device_id_type=MESH)
    for o in others:
        pl.semaphore_signal(barrier, inc=1, device_id=dev(r, z, o), device_id_type=MESH)

    @pl.when(r != z)
    def _():
        for o in range(4):
            pl.semaphore_signal(barrier, inc=1, device_id=dev(z, r, o), device_id_type=MESH)

    def keep(i, j):
        bi, bj = r * 8 + i, c * 2 + j
        return ((pat[bi, bj] != 0) | (bi == bj)) & (bj >= bi), bi == bj

    for i in range(8):
        for j in range(2):
            kept, same = keep(i, j)
            block = dens[pl.ds(i * BLK, BLK), pl.ds(j * BLK, BLK)].astype(jnp.float32)
            block = jnp.where(kept, block, jnp.zeros_like(block))
            tbuf[pl.ds(i * BLK, BLK), pl.ds(j * BLK, BLK)] = block.astype(jnp.bfloat16)
            strict = jnp.where(same, jnp.zeros_like(block), block)
            ttbuf[pl.ds(j * BLK, BLK), pl.ds(i * BLK, BLK)] = strict.T.astype(jnp.bfloat16)

    pl.semaphore_wait(barrier, 7 + 4 * (r != z).astype(jnp.int32))

    def quarter(i):
        return pl.ds(pl.multiple_of(i * TILE, TILE), TILE)

    def row_slot(k):
        return rowb.at[:, quarter(k)]

    def col_slot(k):
        return colb.at[quarter(k), :]

    def intra(o):
        return copy(
            tbuf.at[quarter(o), :], colb.at[quarter(r), quarter(s)],
            intra_s.at[o], intra_r.at[s], dev(r, z, o),
        )

    def intra_in(o):
        return copy(
            tbuf.at[quarter(o), :], colb.at[quarter(r), quarter(o)],
            intra_s.at[o], intra_r.at[o], dev(r, z, o),
        )

    def mirror_row(o):
        return copy(
            ttbuf.at[:, quarter(o)], rowb.at[quarter(s), quarter(r)],
            mirr_s.at[o], mirr_r.at[s], dev(z, r, o),
        )

    def mirror_row_in(o):
        return copy(
            ttbuf.at[:, quarter(o)], rowb.at[quarter(o), quarter(z)],
            mirr_s.at[o], mirr_r.at[o], dev(z, r, o),
        )

    def mirror_col(slot):
        return copy(ttbuf, col_slot(slot), mirc_s, mirc_r, dev(z, r, s))

    @pl.when(upper)
    def _():
        mirror_col(z).start()
        for o in range(4):
            mirror_row(o).start()
        for o in others:
            intra(o).start()
        rowb[:, quarter(z)] = tbuf[...]
        colb[quarter(r), quarter(s)] = tbuf[quarter(s), :]
        for o in others:
            intra_in(o).wait_recv()

    @pl.when(diag)
    def _():
        for o in others:
            mirror_row(o).start()
        for o in others:
            intra(o).start()
        rowb[quarter(s), quarter(z)] = ttbuf[:, quarter(s)]
        colb[quarter(r), quarter(s)] = tbuf[quarter(s), :]
        for o in others:
            mirror_row_in(o).wait_recv()
            intra_in(o).wait_recv()
        rowb[:, quarter(z)] = rowb[:, quarter(z)] + tbuf[...]
        colb[quarter(r), :] = colb[quarter(r), :] + ttbuf[...]

    @pl.when(lower)
    def _():
        mirror_col(r).wait_recv()
        for o in range(4):
            mirror_row_in(o).wait_recv()

    away, home = (1 - p) * 2, p * 2

    def col_quarter(ch):
        return (away if ch < 2 else home) + ch % 2

    def ring_copy(ring, d, ch, item):
        t_sem = item[1]
        k = item[0]
        if ring == 0:
            ref = rowb.at[pl.ds(ch * TILE, TILE), quarter(k)]
        else:
            ref = colb.at[quarter(k), quarter(col_quarter(ch))]
        return copy(
            ref, ref, ring_s.at[ring, d, ch, t_sem - 1], ring_r.at[ring, d, ch, t_sem - 1],
            neighbours[ring][d],
        )

    def item_at(ring, d, dist):
        pos = z if ring == 0 else h
        pos = lax.rem(pos + (8 - dist if d == 0 else dist), 8)
        return pos if ring == 0 else ring_row(pos, p)

    def is_sent(d, ch, t):
        return t <= 3 or ch % 2 == d

    def send(ring, d, ch, t):
        return ring_copy(ring, d, ch, (item_at(ring, d, t - 1), t))

    def recv(ring, d, ch, t):
        return ring_copy(ring, d, ch, (item_at(ring, d, t), t))

    ringdirs = [(a, d) for a in range(2) for d in range(2)]

    def step(ch, t):
        for a, d in ringdirs:
            if not is_sent(d, ch, t):
                continue
            if t > 1:
                recv(a, d, ch, t - 1).wait_recv()
            send(a, d, ch, t).start()

    def drain(ch):
        for a, d in ringdirs:
            if is_sent(d, ch, 4):
                recv(a, d, ch, 4).wait_recv()
            else:
                recv(a, d, ch, 3).wait_recv()

    def pair_round(c0, c1, extra):
        for t in (2, 3, 4):
            step(c0, t)
            step(c1, t)
        for e in extra:
            step(e, 1)
        drain(c0)
        drain(c1)

    def matmul(m0, nq):
        cols = quarter(nq)

        def body(i, carry):
            rows = pl.ds(pl.multiple_of(m0 + i * TILE, TILE), TILE)
            part[rows, cols] = jnp.dot(
                rowb[rows, :], colb[:, cols], preferred_element_type=jnp.float32
            )
            return carry

        lax.fori_loop(0, 2, body, 0)

    sibling = dev(r, z, lax.rem(s, 2) * 0 + 2 * p + (1 - q))
    partner = dev(r, z, 2 * (1 - p) + q)
    half = SUPER // 2

    def sib_away(i):
        rows = pl.ds(i * half, half)
        return copy(
            part.at[rows, quarter(away + 1 - q)], sibb.at[rows, pl.ds(0, TILE)],
            sib_s.at[i], sib_r.at[i], sibling,
        )

    def sib_home():
        return copy(
            part.at[:, quarter(home + 1 - q)], sibb.at[:, pl.ds(TILE, TILE)],
            sib_s.at[2], sib_r.at[2], sibling,
        )

    def y_copy(i):
        rows = pl.ds(i * half, half)
        return copy(ysend.at[rows, :], yrecv.at[rows, :], y_s.at[i], y_r.at[i], partner)

    def away_part(i):
        matmul(i * half, away + 1 - q)
        sib_away(i).start()
        matmul(i * half, away + q)
        sib_away(i).wait_recv()
        rows = pl.ds(i * half, half)
        ysend[rows, :] = part[rows, quarter(away + q)] + sibb[rows, pl.ds(0, TILE)]
        y_copy(i).start()

    step(0, 1)
    step(1, 1)
    pair_round(0, 1, (2, 3))
    away_part(0)
    pair_round(2, 3, ())
    away_part(1)
    for i in range(2):
        matmul(i * half, home + 1 - q)
    sib_home().start()
    for i in range(2):
        matmul(i * half, home + q)
    sib_home().wait_recv()
    for i in range(2):
        y_copy(i).wait_recv()
    for i in range(8):
        rows = pl.ds(i * BLK, BLK)
        value = part[rows, quarter(home + q)] + sibb[rows, pl.ds(TILE, TILE)] + yrecv[rows, :]
        for j in range(2):
            kept, _same = keep(i, j)
            block = value[:, j * BLK:(j + 1) * BLK]
            block = jnp.where(kept, block, jnp.zeros_like(block))
            out[rows, pl.ds(j * BLK, BLK)] = block.astype(jnp.bfloat16)

    for ch in range(CHUNKS):
        for t in (1, 2, 3, 4):
            for a, d in ringdirs:
                if is_sent(d, ch, t):
                    send(a, d, ch, t).wait_send()
    for i in range(2):
        sib_away(i).wait_send()
        y_copy(i).wait_send()
    sib_home().wait_send()

    @pl.when(upper)
    def _():
        mirror_col(z).wait_send()
        for o in range(4):
            mirror_row(o).wait_send()
        for o in others:
            intra(o).wait_send()

    @pl.when(diag)
    def _():
        for o in others:
            mirror_row(o).wait_send()
            intra(o).wait_send()


def square_tile(pattern, density):
    dma = pltpu.SemaphoreType.DMA
    return pl.pallas_call(
        kernel,
        out_shape=jax.ShapeDtypeStruct(density.shape, jnp.bfloat16),
        in_specs=[
            pl.BlockSpec(memory_space=pltpu.SMEM),
            pl.BlockSpec(memory_space=pltpu.VMEM),
        ],
        out_specs=pl.BlockSpec(memory_space=pltpu.VMEM),
        scratch_shapes=[
            pltpu.VMEM((SUPER, TILE), jnp.bfloat16),
            pltpu.VMEM((TILE, SUPER), jnp.bfloat16),
            pltpu.VMEM((SUPER, NSUP * TILE), jnp.bfloat16),
            pltpu.VMEM((NSUP * TILE, SUPER), jnp.bfloat16),
            pltpu.VMEM((SUPER, SUPER), jnp.float32),
            pltpu.VMEM((SUPER, 2 * TILE), jnp.float32),
            pltpu.VMEM((SUPER, TILE), jnp.float32),
            pltpu.VMEM((SUPER, TILE), jnp.float32),
            dma((2, 2, CHUNKS, 4)), dma((2, 2, CHUNKS, 4)),
            dma((4,)), dma((4,)), dma((4,)), dma((4,)), dma, dma,
            dma((3,)), dma((3,)), dma((2,)), dma((2,)),
        ],
        compiler_params=pltpu.CompilerParams(
            collective_id=0, has_side_effects=True, vmem_limit_bytes=40 * 1024 * 1024
        ),
        cost_estimate=pl.CostEstimate(
            flops=2 * SUPER * SUPER * NSUP * TILE, bytes_accessed=16 * 1024 * 1024, transcendentals=0
        ),
    )(pattern, density)


def per_device(density, pattern):
    n_row, n_col = lax.axis_size("row"), lax.axis_size("col")
    row_index, col_index = lax.axis_index("row"), lax.axis_index("col")
    height, width = density.shape
    row_blocks, col_blocks = height // BLK, width // BLK
    block_rows = row_index * row_blocks + jnp.arange(row_blocks)[:, None]
    block_cols = col_index * col_blocks + jnp.arange(col_blocks)[None, :]
    chosen = lax.dynamic_slice(
        pattern, (row_index * row_blocks, col_index * col_blocks), (row_blocks, col_blocks)
    )
    same = block_rows == block_cols
    kept = ((chosen != 0) | same) & (block_cols >= block_rows)
    weight = jnp.where(same, 1.0, jnp.where(kept, 2.0, 0.0)).astype(jnp.float32)
    values = density.astype(jnp.float32)
    rows = row_index * height + lax.broadcasted_iota(jnp.int32, density.shape, 0)
    cols = col_index * width + lax.broadcasted_iota(jnp.int32, density.shape, 1)
    first = jnp.sum(jnp.where(rows == cols, values, 0.0))
    squares = jnp.where(values == 0.0, 0.0, values * values)
    by_block = squares.reshape(row_blocks, BLK, width).sum(axis=1)
    by_block = by_block.reshape(row_blocks, col_blocks, BLK).sum(axis=2)
    second = jnp.sum(jnp.where(kept, weight * by_block, 0.0))
    sums = lax.psum(jnp.stack([first, second]), ("row", "col"))
    square = square_tile(pattern, density)
    return square, sums / (height * n_row)


def solution(mesh):
    return jax.shard_map(
        per_device, mesh=mesh, in_specs=(P("row", "col"), P()),
        out_specs=(P("row", "col"), P()), check_vma=False,
    )
```

time: 553 us -> 266 us (0.48)
  waiting for transfers between devices: 408 us -> 0 us
  Pallas kernels: 0 us -> 178 us
  local copies, waits for them, and re-layouts: 17.7 us -> 3.44 us
  between operations: 13.9 us -> 0.67 us
  matrix products: 12.2 us -> 0 us
  starting transfers between devices: 9.49 us -> 0 us
  other arithmetic: 12 us -> 3.77 us
    psum x1 -> x0, waiting for transfers between devices: 188 us -> none  [spread(): return lax.psum(kept, axis)]
    pallas_call x0 -> x1, Pallas kernels: none -> 178 us  [square_tile(): pl.pallas_call(kernel, out_shape=jax.ShapeDtypeStruct(density.shape, jnp....]
    all_gather x2 -> x0, waiting for transfers between devices: 127 us -> none  [the longest x1 127 us: per_device(): lax.all_gather(own_rows, 'col', axis=1, tiled=True)]
    all_to_all x1 -> x0, waiting for transfers between devices: 93.1 us -> none  [per_device(): lax.all_to_all(outgoing, 'col', split_axis=0, concat_axis=2, tiled=True)]
    dot_general x1 -> x0, matrix products: 12.2 us -> none  [per_device(): jnp.dot(lax.all_gather(own_rows, 'col', axis=1, tiled=True), full_column,...]
    all_to_all x1 -> x0, starting transfers between devices: 9.36 us -> none  [per_device(): lax.all_to_all(outgoing, 'col', split_axis=0, concat_axis=2, tiled=True)]
    broadcast_in_dim x5 -> x0, local copies, waits for them, and re-layouts: 7.32 us -> none  [masked(): jnp.where(block_mask[:, None, :, None], shaped, jnp.zeros_like(shaped))]
  transfers between devices with their start and end apart: 4 -> 0, of which waited for: 3 -> 0; matrix products, arithmetic and copies ran while one was open for 3% -> 0% of each run, Pallas kernels for 0% -> 0%
where the time goes in v1:
time: 266 us; the launch traced here: 261 us
  Pallas kernels  178 us (67%)
  blocking collectives  75.7 us (28%)
  other arithmetic  3.77 us (1%)
  local copies, waits for them, and re-layouts  3.44 us (1%)
    pallas_call x1, Pallas kernels, square_tile(): pl.pallas_call(kernel, out_shape=jax.ShapeDtypeStruct(density.shape, jnp....  178 us
    psum x1, blocking collectives, per_device(): sums = lax.psum(jnp.stack([first, second]), ('row', 'col'))  75.7 us

profile of v1, /device:TPU:88, one launch (start us, length us, event | category | flops | bytes accessed | tf_op | source)
XLA Modules:
  0.0 261.3 jit_solution(4247645308949013777)
XLA Ops:
  0.6 0.0 copy-start
  0.6 1.0 copy-done
  1.7 0.0 copy-start.2
  1.7 0.8 copy-done.2
  2.4 177.7 %shard_map.41 = bf16[1024,256]{1,0:T(8,128)(2,1)S(1)} custom-call(s32[64,64]{1,0:T(8,128)S(1)} %copy-done.2, bf16[1024,256]{1,0:T(8,128)(2,1)S(1)} %copy-done), custom_call_target="tpu_custom_call" | custom-call | flops 4294967296 | bytes 16777216 | tf_op jit(solution)/shard_map/pallas_call | solution.py:302
  180.1 0.0 copy-start.1
  180.2 0.2 bitcast_reduce_fusion
  180.3 0.1 bitcast_reduce_fusion.1
  180.4 0.8 dynamic_slice.3
  181.2 0.1 copy.5
  181.3 0.7 fusion.5
  182.0 0.0 copy-done.1
  182.0 0.9 fusion
  182.9 1.4 pad_maximum_fusion
  184.3 75.7 %psum.7 = f32[2]{0:T(128)S(1)} all-reduce(f32[2]{0:T(128)S(1)} %pad_maximum_fusion), channel_id=1, replica_groups=mesh['row'=8,'col'=32] {'row','col'}, use_global_device_ids=true, to_apply=%region_4.5 | all-reduce | flops 2 | bytes 16 | tf_op jit(solution)/shard_map/psum | solution.py:353
  260.0 0.5 broadcast_multiply_fusion
  260.5 0.8 copy.7
  (4 shorter events, 0.0 us)
Async XLA Ops:
  0.6 1.0 copy-start
  1.7 0.8 copy-start.2
  180.1 1.8 copy-start.1

commit v2 on v0

v2 whole, which is shorter than its diff:
```python
import jax
import jax.numpy as jnp
from jax import lax
from jax.experimental import pallas as pl
from jax.experimental.pallas import tpu as pltpu
from jax.sharding import PartitionSpec as P

BLK = 128
MESH = pl.DeviceIdType.MESH
TILE = 256
SUPER = 1024
NSUP = 8
CHUNKS = 4


def ring_order(r, p):
    x, hi = lax.div(r, 2), lax.rem(r, 2)
    xx = lax.rem(x + 2 * p, 4)
    return xx * (1 - hi) + (7 - xx) * hi


def ring_row(h, p):
    hi = lax.div(h, 4)
    xx = h * (1 - hi) + (7 - h) * hi
    return 2 * lax.rem(xx + 2 * p, 4) + hi


def kernel(
    pat, dens, out, traces,
    tbuf, ttbuf, rowb, colb, part, sibb, ysend, yrecv, tr, trq,
    ring_s, ring_r, inj_s, inj_r, tr_s, tr_r, trq_s, trq_r,
    intra_s, intra_r, mirr_s, mirr_r, sib_s, sib_r, y_s, y_r,
):
    r = lax.axis_index("row")
    c = lax.axis_index("col")
    z, s = lax.div(c, 4), lax.rem(c, 4)
    p, q = lax.div(s, 2), lax.rem(s, 2)
    active, diag = r <= z, r == z

    def dev(r_, z_, s_):
        return (r_, 4 * z_ + s_)

    def copy(src, dst, ssem, rsem, device):
        return pltpu.make_async_remote_copy(
            src_ref=src, dst_ref=dst, send_sem=ssem, recv_sem=rsem,
            device_id=device, device_id_type=MESH,
        )

    def wrap(i):
        return lax.rem(i + 8, 8)

    h = ring_order(r, p)
    neighbours = (
        (dev(r, wrap(z + 1), s), dev(r, wrap(z - 1), s)),
        (dev(ring_row(wrap(h + 1), p), z, s), dev(ring_row(wrap(h - 1), p), z, s)),
    )
    others = [lax.rem(s + d, 4) for d in (1, 2, 3)]

    barrier = pltpu.get_barrier_semaphore()
    for ring in neighbours:
        for device in ring:
            pl.semaphore_signal(barrier, inc=1, device_id=device, device_id_type=MESH)
    for o in others:
        pl.semaphore_signal(barrier, inc=1, device_id=dev(r, z, o), device_id_type=MESH)

    def keep(i, j):
        bi, bj = r * 8 + i, c * 2 + j
        return ((pat[bi, bj] != 0) | (bi == bj)) & (bj >= bi), bi == bj

    def quarter(i):
        return pl.ds(pl.multiple_of(i * TILE, TILE), TILE)

    eye = lax.broadcasted_iota(jnp.int32, (BLK, BLK), 0) == lax.broadcasted_iota(jnp.int32, (BLK, BLK), 1)
    first = jnp.zeros((BLK, BLK), jnp.float32)
    second = jnp.zeros((BLK, BLK), jnp.float32)
    for i in range(8):
        for j in range(2):
            kept, same = keep(i, j)
            block = dens[pl.ds(i * BLK, BLK), pl.ds(j * BLK, BLK)].astype(jnp.float32)
            block = jnp.where(kept, block, jnp.zeros_like(block))
            tbuf[pl.ds(i * BLK, BLK), pl.ds(j * BLK, BLK)] = block.astype(jnp.bfloat16)
            first = first + jnp.where(eye & same, block, jnp.zeros_like(block))
            square = block * block
            second = second + jnp.where(same, square, square + square)

            @pl.when(diag)
            def _():
                strict = jnp.where(same, jnp.zeros_like(block), block)
                ttbuf[pl.ds(j * BLK, BLK), pl.ds(i * BLK, BLK)] = strict.T.astype(jnp.bfloat16)

    tr[0, z, 0:8, :] = first.reshape(BLK // 8, 8, BLK).sum(axis=0)
    tr[0, z, 8:16, :] = second.reshape(BLK // 8, 8, BLK).sum(axis=0)

    pl.semaphore_wait(barrier, 7)

    def intra(o):
        return copy(
            tbuf.at[quarter(o), :], colb.at[quarter(r), quarter(s)],
            intra_s.at[o], intra_r.at[s], dev(r, z, o),
        )

    def intra_in(o):
        return copy(
            tbuf.at[quarter(o), :], colb.at[quarter(r), quarter(o)],
            intra_s.at[o], intra_r.at[o], dev(r, z, o),
        )

    def mirror(o):
        return copy(
            ttbuf.at[:, quarter(o)], rowb.at[quarter(s), quarter(z)],
            mirr_s.at[o], mirr_r.at[s], dev(r, z, o),
        )

    def mirror_in(o):
        return copy(
            ttbuf.at[:, quarter(o)], rowb.at[quarter(o), quarter(z)],
            mirr_s.at[o], mirr_r.at[o], dev(r, z, o),
        )

    away, home = (1 - p) * 2, p * 2
    center = (r, ring_order(z, p))
    pos = (z, h)

    def chunk(ch):
        return quarter((away if ch < 2 else home) + ch % 2)

    def piece(ring, ch, k):
        return rowb.at[chunk(ch), quarter(k)] if ring == 0 else colb.at[quarter(k), chunk(ch)]

    def at(ring, where):
        return wrap(where) if ring == 0 else ring_row(wrap(where), p)

    def item_at(ring, d, dist):
        return at(ring, pos[ring] - dist if d == 0 else pos[ring] + dist)

    def stored(ring, k):
        return k >= r if ring == 0 else k <= z

    def has_hop(d, ch, t):
        return t <= 3 or (t == 4 and ch % 2 == d)

    def hop(ring, d, ch, t, k):
        ref = piece(ring, ch, k)
        return copy(
            ref, ref, ring_s.at[ring, d, ch, t - 1], ring_r.at[ring, d, ch, t - 1],
            neighbours[ring][d],
        )

    ringdirs = [(a, d) for a in range(2) for d in range(2)]

    def tr_hop(ring, d, t, k):
        ref = tr.at[ring, k]
        return copy(ref, ref, tr_s.at[ring, d, t - 1], tr_r.at[ring, d, t - 1], neighbours[ring][d])

    def own(ring, chs):
        @pl.when(active)
        def _():
            for ch in chs:
                for d in range(2):
                    hop(ring, d, ch, 1, item_at(ring, d, 0)).start()

    def tr_own(ring):
        for d in range(2):
            tr_hop(ring, d, 1, item_at(ring, d, 0)).start()

    def natural(chs, t):
        for ch in chs:
            for ring, d in ringdirs:
                if not has_hop(d, ch, t):
                    continue
                k = item_at(ring, d, t)

                @pl.when(stored(ring, k))
                def _():
                    hop(ring, d, ch, t, k).wait_recv()
                    if has_hop(d, ch, t + 1):
                        hop(ring, d, ch, t + 1, k).start()

    def tr_step(ring, t):
        for d in range(2):
            if has_hop(d, 0, t):
                k = item_at(ring, d, t)
                tr_hop(ring, d, t, k).wait_recv()
                if has_hop(d, 0, t + 1):
                    tr_hop(ring, d, t + 1, k).start()

    def mirrored(ring, e, d):
        source = (ring_order(r, p), z)[ring]
        k = at(1 - ring, source - d if e == 0 else source + d)
        return k, (k < r if ring == 0 else k > z)

    def along(ring, ch):
        return wrap(pos[ring] - center[ring] if ch % 2 == 0 else center[ring] - pos[ring])

    def last(ring, ch):
        if ring == 1:
            return jnp.where(z > 0, 7, 0)
        return 7 - r if ch % 2 == 0 else jnp.where(r < 7, 7, 0)

    def inj_hop(ring, e, d, ch, k):
        ref = piece(ring, ch, k)
        return copy(
            ref, ref, inj_s.at[ring, e, d - 1, ch], inj_r.at[ring, e, d - 1, ch],
            neighbours[ring][ch % 2],
        )

    def inject(chs, t):
        for ch in chs:
            for ring in range(2):
                j = along(ring, ch)
                end = last(ring, ch)
                d = t - j
                for e in range(2):
                    k, exists = mirrored(ring, e, d)
                    here = exists & (d >= 1) & (d <= (3 if e else 4)) & (j <= end)

                    @pl.when(here & (j > 0))
                    def _():
                        inj_hop(ring, e, d, ch, k).wait_recv()

                    if t <= 4:

                        @pl.when(here & (j == 0))
                        def _():
                            if ring == 0:
                                rowb[chunk(ch), quarter(k)] = colb[quarter(k), chunk(ch)].T
                            else:
                                colb[quarter(k), chunk(ch)] = rowb[chunk(ch), quarter(k)].T

                    @pl.when(here & (j < end))
                    def _():
                        inj_hop(ring, e, d, ch, k).start()

    def step(chs, t):
        if t <= 4:
            natural(chs, t)
        inject(chs, t)

    def matmul(m0, nq):
        cols = quarter(nq)

        def body(i, carry):
            rows = pl.ds(pl.multiple_of(m0 + i * TILE, TILE), TILE)
            part[rows, cols] = jnp.dot(
                rowb[rows, :], colb[:, cols], preferred_element_type=jnp.float32
            )
            return carry

        lax.fori_loop(0, 2, body, 0)

    sibling = dev(r, z, 2 * p + (1 - q))
    partner = dev(r, z, 2 * (1 - p) + q)
    half = SUPER // 2
    starts = (away * TILE, home * TILE)

    def rows_of(i):
        return pl.ds(pl.multiple_of(starts[i], half), half)

    def sib_away(i):
        rows = rows_of(i)
        return copy(
            part.at[rows, quarter(away + 1 - q)], sibb.at[rows, pl.ds(0, TILE)],
            sib_s.at[i], sib_r.at[i], sibling,
        )

    def sib_home():
        return copy(
            part.at[:, quarter(home + 1 - q)], sibb.at[:, pl.ds(TILE, TILE)],
            sib_s.at[2], sib_r.at[2], sibling,
        )

    def y_copy(i):
        rows = rows_of(i)
        return copy(ysend.at[rows, :], yrecv.at[rows, :], y_s.at[i], y_r.at[i], partner)

    def y_in(i):
        rows = rows_of(1 - i)
        return copy(ysend.at[rows, :], yrecv.at[rows, :], y_s.at[i], y_r.at[i], partner)

    def away_1(i):
        @pl.when(active)
        def _():
            matmul(starts[i], away + 1 - q)
            sib_away(i).start()

    def away_2(i):
        @pl.when(active)
        def _():
            matmul(starts[i], away + q)

    def away_3(i):
        @pl.when(active)
        def _():
            sib_away(i).wait_recv()
            rows = rows_of(i)
            ysend[rows, :] = part[rows, quarter(away + q)] + sibb[rows, pl.ds(0, TILE)]
            y_copy(i).start()

    def trq_copy(o):
        return copy(trq.at[s], trq.at[s], trq_s.at[o], trq_r.at[s], dev(r, z, o))

    def trq_in(o):
        return copy(trq.at[o], trq.at[o], trq_s.at[o], trq_r.at[o], dev(r, z, o))

    def total(ref, n):
        value = ref[0]
        for i in range(1, n):
            value = value + ref[i]
        return value

    @pl.when(active)
    def _():
        for o in others:
            intra(o).start()

    @pl.when(r < z)
    def _():
        rowb[:, quarter(z)] = tbuf[...]
        colb[quarter(r), quarter(s)] = tbuf[quarter(s), :]
        for o in others:
            intra_in(o).wait_recv()

    @pl.when(diag)
    def _():
        for o in others:
            mirror(o).start()
        rowb[quarter(s), quarter(z)] = ttbuf[:, quarter(s)]
        colb[quarter(r), quarter(s)] = tbuf[quarter(s), :]
        for o in others:
            mirror_in(o).wait_recv()
            intra_in(o).wait_recv()
        rowb[:, quarter(z)] = rowb[:, quarter(z)] + tbuf[...]
        colb[quarter(r), :] = colb[quarter(r), :] + ttbuf[...]

    tr_own(0)
    for ring in range(2):
        own(ring, (0, 1))
    for u in range(1, 16):
        if u == 3:
            for ring in range(2):
                own(ring, (2, 3))
        if u <= 11:
            step((0, 1), u)
        if u <= 4:
            tr_step(0, u)
        if u >= 5:
            step((2, 3), u - 4)
        if u == 5:
            tr[1, r] = total(tr.at[0], 8)
            tr_own(1)
        if 6 <= u <= 9:
            tr_step(1, u - 5)
        if u == 10:
            trq[s] = total(tr.at[1], 8)
            for o in others:
                trq_copy(o).start()
        if u == 12:
            away_1(0)
        if u == 13:
            away_2(0)
        if u == 14:
            away_3(0)
    away_1(1)
    away_2(1)
    away_3(1)

    @pl.when(active)
    def _():
        for i in range(2):
            matmul(i * half, home + 1 - q)
        sib_home().start()
        for i in range(2):
            matmul(i * half, home + q)

    for o in others:
        trq_in(o).wait_recv()
    sums = total(trq, 4)
    traces[0] = jnp.sum(sums[0:8, :]) / (NSUP * SUPER)
    traces[1] = jnp.sum(sums[8:16, :]) / (NSUP * SUPER)

    @pl.when(active)
    def _():
        sib_home().wait_recv()
        for i in range(2):
            y_in(i).wait_recv()
        for i in range(8):
            rows = pl.ds(i * BLK, BLK)
            value = part[rows, quarter(home + q)] + sibb[rows, pl.ds(TILE, TILE)] + yrecv[rows, :]
            for j in range(2):
                kept, _same = keep(i, j)
                block = value[:, j * BLK:(j + 1) * BLK]
                block = jnp.where(kept, block, jnp.zeros_like(block))
                out[rows, pl.ds(j * BLK, BLK)] = block.astype(jnp.bfloat16)

    @pl.when(r > z)
    def _():
        out[...] = jnp.zeros_like(out)

    for ring, d in ringdirs:
        for t in (1, 2, 3, 4):
            k = item_at(ring, d, t - 1)
            if has_hop(d, 0, t):
                tr_hop(ring, d, t, k).wait_send()

            @pl.when(stored(ring, k))
            def _():
                for ch in range(CHUNKS):
                    if has_hop(d, ch, t):
                        hop(ring, d, ch, t, k).wait_send()

    for ch in range(CHUNKS):
        for ring in range(2):
            for e in range(2):
                for d in range(1, 4 if e else 5):
                    k, exists = mirrored(ring, e, d)

                    @pl.when(exists & (along(ring, ch) < last(ring, ch)))
                    def _():
                        inj_hop(ring, e, d, ch, k).wait_send()

    for o in others:
        trq_copy(o).wait_send()

    @pl.when(active)
    def _():
        for i in range(2):
            sib_away(i).wait_send()
            y_copy(i).wait_send()
        sib_home().wait_send()
        for o in others:
            intra(o).wait_send()

    @pl.when(diag)
    def _():
        for o in others:
            mirror(o).wait_send()


def per_device(density, pattern):
    dma = pltpu.SemaphoreType.DMA
    f32, bf16 = jnp.float32, jnp.bfloat16
    return pl.pallas_call(
        kernel,
        out_shape=(
            jax.ShapeDtypeStruct(density.shape, bf16),
            jax.ShapeDtypeStruct((2,), f32),
        ),
        in_specs=[
            pl.BlockSpec(memory_space=pltpu.SMEM),
            pl.BlockSpec(memory_space=pltpu.VMEM),
        ],
        out_specs=(
            pl.BlockSpec(memory_space=pltpu.VMEM),
            pl.BlockSpec(memory_space=pltpu.SMEM),
        ),
        scratch_shapes=[
            pltpu.VMEM((SUPER, TILE), bf16),
            pltpu.VMEM((TILE, SUPER), bf16),
            pltpu.VMEM((SUPER, NSUP * TILE), bf16),
            pltpu.VMEM((NSUP * TILE, SUPER), bf16),
            pltpu.VMEM((SUPER, SUPER), f32),
            pltpu.VMEM((SUPER, 2 * TILE), f32),
            pltpu.VMEM((SUPER, TILE), f32),
            pltpu.VMEM((SUPER, TILE), f32),
            pltpu.VMEM((2, NSUP, 16, BLK), f32),
            pltpu.VMEM((4, 16, BLK), f32),
            dma((2, 2, CHUNKS, 4)), dma((2, 2, CHUNKS, 4)),
            dma((2, 2, 4, CHUNKS)), dma((2, 2, 4, CHUNKS)),
            dma((2, 2, 4)), dma((2, 2, 4)), dma((4,)), dma((4,)),
            dma((4,)), dma((4,)), dma((4,)), dma((4,)),
            dma((3,)), dma((3,)), dma((2,)), dma((2,)),
        ],
        compiler_params=pltpu.CompilerParams(
            collective_id=0, has_side_effects=True, vmem_limit_bytes=40 * 1024 * 1024
        ),
        cost_estimate=pl.CostEstimate(
            flops=2 * SUPER * SUPER * NSUP * TILE, bytes_accessed=2 * 1024 * 1024, transcendentals=0
        ),
    )(pattern, density)


def solution(mesh):
    return jax.shard_map(
        per_device, mesh=mesh, in_specs=(P("row", "col"), P()),
        out_specs=(P("row", "col"), P()), check_vma=False,
    )
```

time: 553 us -> 148 us (0.27)
  the two profiles are of different devices: /device:TPU:88 before, /device:TPU:40 now
where the time goes in v2:
time: 148 us; the launch traced here: 147 us
  Pallas kernels  144 us (97%)
  local copies, waits for them, and re-layouts  3.1 us (2%)
    pallas_call x1, Pallas kernels, per_device(): pl.pallas_call(kernel, out_shape=(jax.ShapeDtypeStruct(density.shape, bf1...  144 us
    unnamed x6, local copies, waits for them, and re-layouts  3.1 us

profile of v2, /device:TPU:40, one launch (start us, length us, event | category | flops | bytes accessed | tf_op | source)
XLA Modules:
  0.0 147.3 jit_solution(8633671817899500315)
XLA Ops:
  0.6 0.0 copy-start
  0.6 1.0 copy-done
  1.7 0.0 copy-start.1
  1.7 0.8 copy-done.1
  2.4 143.6 %shard_map.41 = (bf16[1024,256]{1,0:T(8,128)(2,1)S(1)}, f32[2]{0:T(128)S(1)}) custom-call(s32[64,64]{1,0:T(8,128)S(1)} %copy-done.1, bf16[1024,256]{1,0:T(8,128)(2,1)S(1)} %copy-done), custom_call_target="tpu_custom_call" | custom-call | flops 4294967296 | bytes 2097152 | tf_op jit(solution)/shard_map/pallas_call | solution.py:442
  146.0 0.8 copy.6
  146.8 0.5 copy.7
Async XLA Ops:
  0.6 1.0 copy-start
  1.7 0.8 copy-start.1

commit v3 on v2

--- a/solution.py
+++ b/solution.py
@@ -11,6 +11,7 @@
 SUPER = 1024
 NSUP = 8
 CHUNKS = 4
+REACH = 3
 
 
 def ring_order(r, p):
@@ -25,10 +26,76 @@
     return 2 * lax.rem(xx + 2 * p, 4) + hi
 
 
+def plain_order(p):
+    rows = []
+    for h in range(8):
+        hi = h // 4
+        xx = 7 - h if hi else h
+        rows.append(2 * ((xx + 2 * p) % 4) + hi)
+    return rows
+
+
+def chains(ring, p, center, parity):
+    order = plain_order(p) if ring else list(range(8))
+    start = order.index(center)
+
+    def needs(i):
+        other = order[(start + i) % 8]
+        return other < center if ring else other > center
+
+    offsets = [i for i in range(1, 8) if needs(i)]
+    n = len(offsets)
+    split = n // 2 if n >= 4 else (0 if parity else n)
+    table, firsts = {}, []
+    for sign, goals in ((1, offsets[:split]), (-1, [8 - i for i in reversed(offsets[split:])])):
+        nodes, now = [], 0
+        for goal in goals:
+            while goal - now > REACH:
+                now += REACH
+                nodes.append(now)
+            nodes.append(goal)
+            now = goal
+        places = [order[(start + sign * i) % 8] for i in nodes]
+        for depth, place in enumerate(places):
+            assert place not in table
+            following = places[depth + 1] if depth + 1 < len(places) else place
+            table[place] = (depth + 1, following)
+        firsts.append(places[0] if places else center)
+    table[center] = (0, firsts[0])
+    return table, firsts[1]
+
+
+def packed(ring, p, parity):
+    depths, nexts, seconds = [], [], []
+    for center in range(8):
+        table, second = chains(ring, p, center, parity)
+        depths.append(sum(table.get(i, (0, i))[0] * 8**i for i in range(8)))
+        nexts.append(sum(table.get(i, (0, i))[1] * 8**i for i in range(8)))
+        seconds.append(second)
+    return depths, nexts, seconds
+
+
+DEEPEST = max(
+    depth
+    for ring in range(2)
+    for p in range(2)
+    for center in range(8)
+    for parity in range(2)
+    for depth, _next in chains(ring, p, center, parity)[0].values()
+)
+
+
+def pick(values, index):
+    result = jnp.int32(values[0])
+    for i, value in enumerate(values):
+        result = jnp.where(index == i, jnp.int32(value), result)
+    return result
+
+
 def kernel(
     pat, dens, out, traces,
     tbuf, ttbuf, rowb, colb, part, sibb, ysend, yrecv, tr, trq,
-    ring_s, ring_r, inj_s, inj_r, tr_s, tr_r, trq_s, trq_r,
+    ring_s, ring_r, inj_s, inj_l, inj_r, tr_s, tr_r, trq_s, trq_r,
     intra_s, intra_r, mirr_s, mirr_r, sib_s, sib_r, y_s, y_r,
 ):
     r = lax.axis_index("row")
@@ -57,8 +124,8 @@
     others = [lax.rem(s + d, 4) for d in (1, 2, 3)]
 
     barrier = pltpu.get_barrier_semaphore()
-    for ring in neighbours:
-        for device in ring:
+    for i in range(1, 8):
+        for device in (dev(r, wrap(z + i), s), dev(wrap(r + i), z, s)):
             pl.semaphore_signal(barrier, inc=1, device_id=device, device_id_type=MESH)
     for o in others:
         pl.semaphore_signal(barrier, inc=1, device_id=dev(r, z, o), device_id_type=MESH)
@@ -91,7 +158,7 @@
     tr[0, z, 0:8, :] = first.reshape(BLK // 8, 8, BLK).sum(axis=0)
     tr[0, z, 8:16, :] = second.reshape(BLK // 8, 8, BLK).sum(axis=0)
 
-    pl.semaphore_wait(barrier, 7)
+    pl.semaphore_wait(barrier, 17)
 
     def intra(o):
         return copy(
@@ -118,7 +185,6 @@
         )
 
     away, home = (1 - p) * 2, p * 2
-    center = (r, ring_order(z, p))
     pos = (z, h)
 
     def chunk(ch):
@@ -152,11 +218,32 @@
         ref = tr.at[ring, k]
         return copy(ref, ref, tr_s.at[ring, d, t - 1], tr_r.at[ring, d, t - 1], neighbours[ring][d])
 
+    ahead = [
+        [
+            [r <= wrap(z + i) if d == 0 else r <= wrap(z - i) for i in range(5)],
+            [at(1, h + i) <= z if d == 0 else at(1, h - i) <= z for i in range(5)],
+        ]
+        for d in range(2)
+    ]
+
+    def served(ring, d, i, j):
+        result = ahead[d][ring][i]
+        for k in range(i + 1, j + 1):
+            result = result | ahead[d][ring][k]
+        return result
+
+    def goes(ring, d, ch, t):
+        return served(ring, d, 1, (4 if ch % 2 == d else 3) - t + 1)
+
+    def comes(ring, d, ch, t):
+        return served(ring, d, 0, (4 if ch % 2 == d else 3) - t)
+
     def own(ring, chs):
-        @pl.when(active)
-        def _():
-            for ch in chs:
-                for d in range(2):
+        for ch in chs:
+            for d in range(2):
+
+                @pl.when(active & goes(ring, d, ch, 1))
+                def _():
                     hop(ring, d, ch, 1, item_at(ring, d, 0)).start()
 
     def tr_own(ring):
@@ -170,10 +257,14 @@
                     continue
                 k = item_at(ring, d, t)
 
-                @pl.when(stored(ring, k))
+                @pl.when(stored(ring, k) & comes(ring, d, ch, t))
                 def _():
                     hop(ring, d, ch, t, k).wait_recv()
-                    if has_hop(d, ch, t + 1):
+
+                if has_hop(d, ch, t + 1):
+
+                    @pl.when(stored(ring, k) & goes(ring, d, ch, t + 1))
+                    def _():
                         hop(ring, d, ch, t + 1, k).start()
 
     def tr_step(ring, t):
@@ -189,47 +280,60 @@
         k = at(1 - ring, source - d if e == 0 else source + d)
         return k, (k < r if ring == 0 else k > z)
 
-    def along(ring, ch):
-        return wrap(pos[ring] - center[ring] if ch % 2 == 0 else center[ring] - pos[ring])
-
-    def last(ring, ch):
-        if ring == 1:
-            return jnp.where(z > 0, 7, 0)
-        return 7 - r if ch % 2 == 0 else jnp.where(r < 7, 7, 0)
-
-    def inj_hop(ring, e, d, ch, k):
+    me = (z, r)
+    centers = (r, z)
+    route = []
+    for ring in range(2):
+        for parity in range(2):
+            found = [packed(ring, i, parity) for i in range(1 + ring)]
+            fields = []
+            for field in range(3):
+                value = pick(found[0][field], centers[ring])
+                if ring:
+                    value = jnp.where(p == 0, value, pick(found[1][field], centers[ring]))
+                fields.append(value)
+            power = pick([8**i for i in range(8)], me[ring])
+            fields[:2] = [lax.rem(lax.div(value, power), 8) for value in fields[:2]]
+            route.append(fields)
+
+    def inj_hop(ring, e, d, ch, k, to, sem):
         ref = piece(ring, ch, k)
         return copy(
-            ref, ref, inj_s.at[ring, e, d - 1, ch], inj_r.at[ring, e, d - 1, ch],
-            neighbours[ring][ch % 2],
+            ref, ref, sem.at[ring, e, d - 1, ch], inj_r.at[ring, e, d - 1, ch],
+            dev(r, to, s) if ring == 0 else dev(to, z, s),
         )
 
     def inject(chs, t):
         for ch in chs:
             for ring in range(2):
-                j = along(ring, ch)
-                end = last(ring, ch)
-                d = t - j
+                depth, to, second = route[2 * ring + ch % 2]
+                d = t - depth
                 for e in range(2):
                     k, exists = mirrored(ring, e, d)
-                    here = exists & (d >= 1) & (d <= (3 if e else 4)) & (j <= end)
-
-                    @pl.when(here & (j > 0))
+                    here = exists & (d >= 1) & (d <= (3 if e else 4))
+
+                    @pl.when(here & (depth > 0))
                     def _():
-                        inj_hop(ring, e, d, ch, k).wait_recv()
+                        inj_hop(ring, e, d, ch, k, to, inj_s).wait_recv()
 
                     if t <= 4:
 
-                        @pl.when(here & (j == 0))
+                        @pl.when(here & diag)
                         def _():
                             if ring == 0:
                                 rowb[chunk(ch), quarter(k)] = colb[quarter(k), chunk(ch)].T
                             else:
                                 colb[quarter(k), chunk(ch)] = rowb[chunk(ch), quarter(k)].T
 
-                    @pl.when(here & (j < end))
+                    @pl.when(here & (to != me[ring]) & (diag | (depth > 0)))
                     def _():
-                        inj_hop(ring, e, d, ch, k).start()
+                        inj_hop(ring, e, d, ch, k, to, inj_s).start()
+
+                    if t <= 4:
+
+                        @pl.when(here & diag & (second != me[ring]))
+                        def _():
+                            inj_hop(ring, e, d, ch, k, second, inj_l).start()
 
     def step(chs, t):
         if t <= 4:
@@ -316,6 +420,7 @@
     @pl.when(r < z)
     def _():
         rowb[:, quarter(z)] = tbuf[...]
+        own(0, (0, 1))
         colb[quarter(r), quarter(s)] = tbuf[quarter(s), :]
         for o in others:
             intra_in(o).wait_recv()
@@ -330,16 +435,17 @@
             mirror_in(o).wait_recv()
             intra_in(o).wait_recv()
         rowb[:, quarter(z)] = rowb[:, quarter(z)] + tbuf[...]
+        own(0, (0, 1))
         colb[quarter(r), :] = colb[quarter(r), :] + ttbuf[...]
 
+    own(1, (0, 1))
     tr_own(0)
-    for ring in range(2):
-        own(ring, (0, 1))
-    for u in range(1, 16):
+    end = 4 + DEEPEST
+    for u in range(1, end + 5):
         if u == 3:
             for ring in range(2):
                 own(ring, (2, 3))
-        if u <= 11:
+        if u <= end:
             step((0, 1), u)
         if u <= 4:
             tr_step(0, u)
@@ -354,11 +460,11 @@
             trq[s] = total(tr.at[1], 8)
             for o in others:
                 trq_copy(o).start()
-        if u == 12:
+        if u == end + 1:
             away_1(0)
-        if u == 13:
+        if u == end + 2:
             away_2(0)
-        if u == 14:
+        if u == end + 3:
             away_3(0)
     away_1(1)
     away_2(1)
@@ -402,21 +508,27 @@
             if has_hop(d, 0, t):
                 tr_hop(ring, d, t, k).wait_send()
 
-            @pl.when(stored(ring, k))
-            def _():
-                for ch in range(CHUNKS):
-                    if has_hop(d, ch, t):
+            for ch in range(CHUNKS):
+                if has_hop(d, ch, t):
+
+                    @pl.when(stored(ring, k) & goes(ring, d, ch, t))
+                    def _():
                         hop(ring, d, ch, t, k).wait_send()
 
     for ch in range(CHUNKS):
         for ring in range(2):
+            depth, to, second = route[2 * ring + ch % 2]
             for e in range(2):
                 for d in range(1, 4 if e else 5):
                     k, exists = mirrored(ring, e, d)
 
-                    @pl.when(exists & (along(ring, ch) < last(ring, ch)))
+                    @pl.when(exists & (to != me[ring]) & (diag | (depth > 0)))
                     def _():
-                        inj_hop(ring, e, d, ch, k).wait_send()
+                        inj_hop(ring, e, d, ch, k, to, inj_s).wait_send()
+
+                    @pl.when(exists & diag & (second != me[ring]))
+                    def _():
+                        inj_hop(ring, e, d, ch, k, second, inj_l).wait_send()
 
     for o in others:
         trq_copy(o).wait_send()
@@ -465,7 +577,7 @@
             pltpu.VMEM((2, NSUP, 16, BLK), f32),
             pltpu.VMEM((4, 16, BLK), f32),
             dma((2, 2, CHUNKS, 4)), dma((2, 2, CHUNKS, 4)),
-            dma((2, 2, 4, CHUNKS)), dma((2, 2, 4, CHUNKS)),
+            dma((2, 2, 4, CHUNKS)), dma((2, 2, 4, CHUNKS)), dma((2, 2, 4, CHUNKS)),
             dma((2, 2, 4)), dma((2, 2, 4)), dma((4,)), dma((4,)),
             dma((4,)), dma((4,)), dma((4,)), dma((4,)),
             dma((3,)), dma((3,)), dma((2,)), dma((2,)),

time: 148 us -> 163 us (1.10)
  the two profiles are of different devices: /device:TPU:40 before, /device:TPU:131 now
where the time goes in v3:
time: 163 us
  Pallas kernels  159 us (98%)
  local copies, waits for them, and re-layouts  3.1 us (2%)
    pallas_call x1, Pallas kernels, per_device(): pl.pallas_call(kernel, out_shape=(jax.ShapeDtypeStruct(density.shape, bf1...  159 us

profile of v3, /device:TPU:131, one launch (start us, length us, event | category | flops | bytes accessed | tf_op | source)
XLA Modules:
  0.0 163.0 jit_solution(18187692073450822398)
XLA Ops:
  0.6 0.0 copy-start
  0.6 1.0 copy-done
  1.7 0.0 copy-start.1
  1.7 0.8 copy-done.1
  2.4 159.3 %shard_map.41 = (bf16[1024,256]{1,0:T(8,128)(2,1)S(1)}, f32[2]{0:T(128)S(1)}) custom-call(s32[64,64]{1,0:T(8,128)S(1)} %copy-done.1, bf16[1024,256]{1,0:T(8,128)(2,1)S(1)} %copy-done), custom_call_target="tpu_custom_call" | custom-call | flops 4294967296 | bytes 2097152 | tf_op jit(solution)/shard_map/pallas_call | solution.py:554
  161.7 0.8 copy.6
  162.5 0.5 copy.7
Async XLA Ops:
  0.6 1.0 copy-start
  1.7 0.8 copy-start.1

commit v4 on v3

--- a/solution.py
+++ b/solution.py
@@ -11,7 +11,7 @@
 SUPER = 1024
 NSUP = 8
 CHUNKS = 4
-REACH = 3
+LAG = 3
 
 
 def ring_order(r, p):
@@ -26,36 +26,47 @@
     return 2 * lax.rem(xx + 2 * p, 4) + hi
 
 
-def plain_order(p):
-    rows = []
-    for h in range(8):
-        hi = h // 4
-        xx = 7 - h if hi else h
-        rows.append(2 * ((xx + 2 * p) % 4) + hi)
-    return rows
+CHAINS = (
+    (
+        (
+            (((), ()), ((), ())),
+            (((7, 6, 5,), (2, 3, 4,)), ((7, 6, 5, 4,), (2, 3,))),
+            (((7, 6, 5,), (3, 4,)), ((7, 6, 5,), (3, 4,))),
+            (((2, 7, 6,), (4, 5,)), ((0, 7, 6, 5,), (4,))),
+            (((), (1, 7, 6, 5,)), ((2, 7,), (5, 6,))),
+            (((), (2, 7, 6,)), ((6, 7,), ())),
+            (((), (3, 2, 7,)), ((7,), ())),
+            (((), ()), ((), ())),
+        ),
+    ),
+    (
+        (
+            (((), ()), ((), ())),
+            (((6, 0,), ()), ((), (2, 0,))),
+            (((), (0, 7, 1,)), ((3, 1,), (6, 0,))),
+            (((4, 2, 0,), (1,)), ((1,), (4, 2, 0,))),
+            (((2, 3, 1,), (0,)), ((2, 0,), (5, 3, 1,))),
+            (((3, 1,), (4, 2, 0,)), ((2, 0, 4,), (3, 1,))),
+            (((7, 5, 3, 1,), (0, 2, 4,)), ((5, 3, 1,), (4, 2, 0,))),
+            (((), ()), ((), ())),
+        ),
+        (
+            (((), ()), ((), ())),
+            (((), (4, 0,)), ((0,), ())),
+            (((), (0, 1,)), ((5, 1, 0,), ())),
+            (((), (1, 0, 2,)), ((2, 0, 1,), ())),
+            (((0, 7, 1, 3,), (2,)), ((2, 6, 0,), (5, 3, 7, 1,))),
+            (((4, 2, 0,), (3, 1,)), ((3, 2, 4,), (1, 0,))),
+            (((4, 2,), (0, 1, 5, 3,)), ((0, 2, 4,), (7, 1, 3, 5,))),
+            (((), ()), ((), ())),
+        ),
+    ),
+)
 
 
 def chains(ring, p, center, parity):
-    order = plain_order(p) if ring else list(range(8))
-    start = order.index(center)
-
-    def needs(i):
-        other = order[(start + i) % 8]
-        return other < center if ring else other > center
-
-    offsets = [i for i in range(1, 8) if needs(i)]
-    n = len(offsets)
-    split = n // 2 if n >= 4 else (0 if parity else n)
     table, firsts = {}, []
-    for sign, goals in ((1, offsets[:split]), (-1, [8 - i for i in reversed(offsets[split:])])):
-        nodes, now = [], 0
-        for goal in goals:
-            while goal - now > REACH:
-                now += REACH
-                nodes.append(now)
-            nodes.append(goal)
-            now = goal
-        places = [order[(start + sign * i) % 8] for i in nodes]
+    for places in CHAINS[ring][p][center][parity]:
         for depth, place in enumerate(places):
             assert place not in table
             following = places[depth + 1] if depth + 1 < len(places) else place
@@ -78,7 +89,7 @@
 DEEPEST = max(
     depth
     for ring in range(2)
-    for p in range(2)
+    for p in range(1 + ring)
     for center in range(8)
     for parity in range(2)
     for depth, _next in chains(ring, p, center, parity)[0].values()
@@ -335,11 +346,6 @@
                         def _():
                             inj_hop(ring, e, d, ch, k, second, inj_l).start()
 
-    def step(chs, t):
-        if t <= 4:
-            natural(chs, t)
-        inject(chs, t)
-
     def matmul(m0, nq):
         cols = quarter(nq)
 
@@ -441,16 +447,20 @@
     own(1, (0, 1))
     tr_own(0)
     end = 4 + DEEPEST
-    for u in range(1, end + 5):
-        if u == 3:
+    for u in range(1, end + LAG + 1):
+        if u == LAG - 1:
             for ring in range(2):
                 own(ring, (2, 3))
+        if u <= 4:
+            natural((0, 1), u)
+        if 1 <= u - LAG <= 4:
+            natural((2, 3), u - LAG)
         if u <= end:
-            step((0, 1), u)
+            inject((0, 1), u)
+        if u > LAG:
+            inject((2, 3), u - LAG)
         if u <= 4:
             tr_step(0, u)
-        if u >= 5:
-            step((2, 3), u - 4)
         if u == 5:
             tr[1, r] = total(tr.at[0], 8)
             tr_own(1)

time: 163 us -> 135 us (0.83)
  the two profiles are of different devices: /device:TPU:131 before, /device:TPU:88 now
where the time goes in v4:
time: 135 us; the launch traced here: 134 us
  Pallas kernels  130 us (96%)
  local copies, waits for them, and re-layouts  3.1 us (2%)
    pallas_call x1, Pallas kernels, per_device(): pl.pallas_call(kernel, out_shape=(jax.ShapeDtypeStruct(density.shape, bf1...  130 us
    unnamed x6, local copies, waits for them, and re-layouts  3.1 us

profile of v4, /device:TPU:88, one launch (start us, length us, event | category | flops | bytes accessed | tf_op | source)
XLA Modules:
  0.0 133.6 jit_solution(3695740772572690535)
XLA Ops:
  0.6 0.0 copy-start
  0.6 1.0 copy-done
  1.7 0.0 copy-start.1
  1.7 0.8 copy-done.1
  2.4 129.9 %shard_map.41 = (bf16[1024,256]{1,0:T(8,128)(2,1)S(1)}, f32[2]{0:T(128)S(1)}) custom-call(s32[64,64]{1,0:T(8,128)S(1)} %copy-done.1, bf16[1024,256]{1,0:T(8,128)(2,1)S(1)} %copy-done), custom_call_target="tpu_custom_call" | custom-call | flops 4294967296 | bytes 2097152 | tf_op jit(solution)/shard_map/pallas_call | solution.py:564
  132.3 0.8 copy.6
  133.1 0.5 copy.7
Async XLA Ops:
  0.6 1.0 copy-start
  1.7 0.8 copy-start.1

commit v5 on v4

--- a/solution.py
+++ b/solution.py
@@ -11,7 +11,7 @@
 SUPER = 1024
 NSUP = 8
 CHUNKS = 4
-LAG = 3
+LAG = 2
 
 
 def ring_order(r, p):
@@ -104,10 +104,11 @@
 
 
 def kernel(
-    pat, dens, out, traces,
-    tbuf, ttbuf, rowb, colb, part, sibb, ysend, yrecv, tr, trq,
+    pat_in, dens_in, out, traces,
+    pat, dens, in_sem,
+    tbuf, rowb, colb, part, sibb, ysend, yrecv, tr, trq,
     ring_s, ring_r, inj_s, inj_l, inj_r, tr_s, tr_r, trq_s, trq_r,
-    intra_s, intra_r, mirr_s, mirr_r, sib_s, sib_r, y_s, y_r,
+    intra_s, intra_r, sib_s, sib_r, y_s, y_r,
 ):
     r = lax.axis_index("row")
     c = lax.axis_index("col")
@@ -140,6 +141,15 @@
             pl.semaphore_signal(barrier, inc=1, device_id=device, device_id_type=MESH)
     for o in others:
         pl.semaphore_signal(barrier, inc=1, device_id=dev(r, z, o), device_id_type=MESH)
+
+    inputs = (
+        pltpu.make_async_copy(pat_in, pat, in_sem.at[0]),
+        pltpu.make_async_copy(dens_in, dens, in_sem.at[1]),
+    )
+    for item in inputs:
+        item.start()
+    for item in inputs:
+        item.wait()
 
     def keep(i, j):
         bi, bj = r * 8 + i, c * 2 + j
@@ -161,11 +171,6 @@
             square = block * block
             second = second + jnp.where(same, square, square + square)
 
-            @pl.when(diag)
-            def _():
-                strict = jnp.where(same, jnp.zeros_like(block), block)
-                ttbuf[pl.ds(j * BLK, BLK), pl.ds(i * BLK, BLK)] = strict.T.astype(jnp.bfloat16)
-
     tr[0, z, 0:8, :] = first.reshape(BLK // 8, 8, BLK).sum(axis=0)
     tr[0, z, 8:16, :] = second.reshape(BLK // 8, 8, BLK).sum(axis=0)
 
@@ -181,18 +186,6 @@
         return copy(
             tbuf.at[quarter(o), :], colb.at[quarter(r), quarter(o)],
             intra_s.at[o], intra_r.at[o], dev(r, z, o),
-        )
-
-    def mirror(o):
-        return copy(
-            ttbuf.at[:, quarter(o)], rowb.at[quarter(s), quarter(z)],
-            mirr_s.at[o], mirr_r.at[s], dev(r, z, o),
-        )
-
-    def mirror_in(o):
-        return copy(
-            ttbuf.at[:, quarter(o)], rowb.at[quarter(o), quarter(z)],
-            mirr_s.at[o], mirr_r.at[o], dev(r, z, o),
         )
 
     away, home = (1 - p) * 2, p * 2
@@ -346,65 +339,51 @@
                         def _():
                             inj_hop(ring, e, d, ch, k, second, inj_l).start()
 
-    def matmul(m0, nq):
+    def matmul(chs, nq):
         cols = quarter(nq)
-
-        def body(i, carry):
-            rows = pl.ds(pl.multiple_of(m0 + i * TILE, TILE), TILE)
+        for ch in chs:
+            rows = chunk(ch)
             part[rows, cols] = jnp.dot(
                 rowb[rows, :], colb[:, cols], preferred_element_type=jnp.float32
             )
-            return carry
-
-        lax.fori_loop(0, 2, body, 0)
 
     sibling = dev(r, z, 2 * p + (1 - q))
     partner = dev(r, z, 2 * (1 - p) + q)
-    half = SUPER // 2
-    starts = (away * TILE, home * TILE)
-
-    def rows_of(i):
-        return pl.ds(pl.multiple_of(starts[i], half), half)
-
-    def sib_away(i):
-        rows = rows_of(i)
+
+    def sib_away(ch):
         return copy(
-            part.at[rows, quarter(away + 1 - q)], sibb.at[rows, pl.ds(0, TILE)],
-            sib_s.at[i], sib_r.at[i], sibling,
+            part.at[chunk(ch), quarter(away + 1 - q)], sibb.at[chunk(ch), pl.ds(0, TILE)],
+            sib_s.at[ch], sib_r.at[ch], sibling,
         )
 
     def sib_home():
         return copy(
             part.at[:, quarter(home + 1 - q)], sibb.at[:, pl.ds(TILE, TILE)],
-            sib_s.at[2], sib_r.at[2], sibling,
-        )
-
-    def y_copy(i):
-        rows = rows_of(i)
-        return copy(ysend.at[rows, :], yrecv.at[rows, :], y_s.at[i], y_r.at[i], partner)
-
-    def y_in(i):
-        rows = rows_of(1 - i)
-        return copy(ysend.at[rows, :], yrecv.at[rows, :], y_s.at[i], y_r.at[i], partner)
-
-    def away_1(i):
+            sib_s.at[CHUNKS], sib_r.at[CHUNKS], sibling,
+        )
+
+    def y_copy(ch):
+        rows = chunk(ch)
+        return copy(ysend.at[rows, :], yrecv.at[rows, :], y_s.at[ch], y_r.at[ch], partner)
+
+    def y_in(ch):
+        rows = chunk((ch + 2) % 4)
+        return copy(ysend.at[rows, :], yrecv.at[rows, :], y_s.at[ch], y_r.at[ch], partner)
+
+    def away_1(ch):
         @pl.when(active)
         def _():
-            matmul(starts[i], away + 1 - q)
-            sib_away(i).start()
-
-    def away_2(i):
+            matmul((ch,), away + 1 - q)
+            sib_away(ch).start()
+            matmul((ch,), away + q)
+
+    def away_2(ch):
         @pl.when(active)
         def _():
-            matmul(starts[i], away + q)
-
-    def away_3(i):
-        @pl.when(active)
-        def _():
-            sib_away(i).wait_recv()
-            rows = rows_of(i)
+            sib_away(ch).wait_recv()
+            rows = chunk(ch)
             ysend[rows, :] = part[rows, quarter(away + q)] + sibb[rows, pl.ds(0, TILE)]
-            y_copy(i).start()
+            y_copy(ch).start()
 
     def trq_copy(o):
         return copy(trq.at[s], trq.at[s], trq_s.at[o], trq_r.at[s], dev(r, z, o))
@@ -418,9 +397,10 @@
             value = value + ref[i]
         return value
 
-    @pl.when(active)
-    def _():
-        for o in others:
+    for o in others:
+
+        @pl.when((r < z) | (diag & (o < s)))
+        def _():
             intra(o).start()
 
     @pl.when(r < z)
@@ -433,32 +413,41 @@
 
     @pl.when(diag)
     def _():
+        block = tbuf[quarter(s), :].astype(jnp.float32)
+        above = lax.broadcasted_iota(jnp.int32, block.shape, 0) // BLK
+        right = lax.broadcasted_iota(jnp.int32, block.shape, 1) // BLK
+        strict = jnp.where(right > above, block, jnp.zeros_like(block))
+        whole = (block + strict.T).astype(jnp.bfloat16)
+        rowb[quarter(s), quarter(z)] = whole
+        colb[quarter(r), quarter(s)] = whole
         for o in others:
-            mirror(o).start()
-        rowb[quarter(s), quarter(z)] = ttbuf[:, quarter(s)]
-        colb[quarter(r), quarter(s)] = tbuf[quarter(s), :]
-        for o in others:
-            mirror_in(o).wait_recv()
-            intra_in(o).wait_recv()
-        rowb[:, quarter(z)] = rowb[:, quarter(z)] + tbuf[...]
+
+            @pl.when(o < s)
+            def _():
+                rowb[quarter(o), quarter(z)] = tbuf[quarter(o), :]
+                colb[quarter(r), quarter(o)] = tbuf[quarter(o), :].T
+
+            @pl.when(o > s)
+            def _():
+                intra_in(o).wait_recv()
+                rowb[quarter(o), quarter(z)] = colb[quarter(r), quarter(o)].T
+
         own(0, (0, 1))
-        colb[quarter(r), :] = colb[quarter(r), :] + ttbuf[...]
 
     own(1, (0, 1))
     tr_own(0)
     end = 4 + DEEPEST
-    for u in range(1, end + LAG + 1):
-        if u == LAG - 1:
-            for ring in range(2):
-                own(ring, (2, 3))
-        if u <= 4:
-            natural((0, 1), u)
-        if 1 <= u - LAG <= 4:
-            natural((2, 3), u - LAG)
-        if u <= end:
-            inject((0, 1), u)
-        if u > LAG:
-            inject((2, 3), u - LAG)
+    for u in range(1, end + LAG * (CHUNKS - 1) + 1):
+        for ch in range(2, CHUNKS):
+            if u == LAG * ch - 1:
+                for ring in range(2):
+                    own(ring, (ch,))
+        for ch in range(CHUNKS):
+            if 1 <= u - LAG * ch <= 4:
+                natural((ch,), u - LAG * ch)
+        for ch in range(CHUNKS):
+            if 1 <= u - LAG * ch <= end:
+                inject((ch,), u - LAG * ch)
         if u <= 4:
             tr_step(0, u)
         if u == 5:
@@ -470,23 +459,24 @@
             trq[s] = total(tr.at[1], 8)
             for o in others:
                 trq_copy(o).start()
-        if u == end + 1:
+        if u == end + LAG:
             away_1(0)
-        if u == end + 2:
+            away_1(1)
+        if u == end + LAG + 1:
             away_2(0)
-        if u == end + 3:
-            away_3(0)
-    away_1(1)
-    away_2(1)
-    away_3(1)
+            away_2(1)
+        if u == end + 2 * LAG:
+            away_1(2)
+        if u == end + 2 * LAG + 1:
+            away_2(2)
+    away_1(3)
+    away_2(3)
 
     @pl.when(active)
     def _():
-        for i in range(2):
-            matmul(i * half, home + 1 - q)
+        matmul(range(CHUNKS), home + 1 - q)
         sib_home().start()
-        for i in range(2):
-            matmul(i * half, home + q)
+        matmul(range(CHUNKS), home + q)
 
     for o in others:
         trq_in(o).wait_recv()
@@ -497,8 +487,8 @@
     @pl.when(active)
     def _():
         sib_home().wait_recv()
-        for i in range(2):
-            y_in(i).wait_recv()
+        for ch in range(CHUNKS):
+            y_in(ch).wait_recv()
         for i in range(8):
             rows = pl.ds(i * BLK, BLK)
             value = part[rows, quarter(home + q)] + sibb[rows, pl.ds(TILE, TILE)] + yrecv[rows, :]
@@ -545,17 +535,16 @@
 
     @pl.when(active)
     def _():
-        for i in range(2):
-            sib_away(i).wait_send()
-            y_copy(i).wait_send()
+        for ch in range(CHUNKS):
+            sib_away(ch).wait_send()
+            y_copy(ch).wait_send()
         sib_home().wait_send()
-        for o in others:
+
+    for o in others:
+
+        @pl.when((r < z) | (diag & (o < s)))
+        def _():
             intra(o).wait_send()
-
-    @pl.when(diag)
-    def _():
-        for o in others:
-            mirror(o).wait_send()
 
 
 def per_device(density, pattern):
@@ -567,17 +556,16 @@
             jax.ShapeDtypeStruct(density.shape, bf16),
             jax.ShapeDtypeStruct((2,), f32),
         ),
-        in_specs=[
-            pl.BlockSpec(memory_space=pltpu.SMEM),
-            pl.BlockSpec(memory_space=pltpu.VMEM),
-        ],
+        in_specs=[pl.BlockSpec(memory_space=pl.ANY)] * 2,
         out_specs=(
             pl.BlockSpec(memory_space=pltpu.VMEM),
             pl.BlockSpec(memory_space=pltpu.SMEM),
         ),
         scratch_shapes=[
+            pltpu.SMEM(pattern.shape, pattern.dtype),
+            pltpu.VMEM(density.shape, density.dtype),
+            dma((2,)),
             pltpu.VMEM((SUPER, TILE), bf16),
-            pltpu.VMEM((TILE, SUPER), bf16),
             pltpu.VMEM((SUPER, NSUP * TILE), bf16),
             pltpu.VMEM((NSUP * TILE, SUPER), bf16),
             pltpu.VMEM((SUPER, SUPER), f32),
@@ -589,8 +577,8 @@
             dma((2, 2, CHUNKS, 4)), dma((2, 2, CHUNKS, 4)),
             dma((2, 2, 4, CHUNKS)), dma((2, 2, 4, CHUNKS)), dma((2, 2, 4, CHUNKS)),
             dma((2, 2, 4)), dma((2, 2, 4)), dma((4,)), dma((4,)),
-            dma((4,)), dma((4,)), dma((4,)), dma((4,)),
-            dma((3,)), dma((3,)), dma((2,)), dma((2,)),
+            dma((4,)), dma((4,)),
+            dma((CHUNKS + 1,)), dma((CHUNKS + 1,)), dma((CHUNKS,)), dma((CHUNKS,)),
         ],
         compiler_params=pltpu.CompilerParams(
             collective_id=0, has_side_effects=True, vmem_limit_bytes=40 * 1024 * 1024

time: 135 us -> 127 us (0.941)
  Pallas kernels: 130 us -> 123 us
    pallas_call x1, Pallas kernels: 130 us -> 123 us  [per_device(): pl.pallas_call(kernel, out_shape=(jax.ShapeDtypeStruct(density.shape, bf1...]
where the time goes in v5:
time: 127 us
  Pallas kernels  123 us (97%)
  local copies, waits for them, and re-layouts  3.1 us (2%)
    pallas_call x1, Pallas kernels, per_device(): pl.pallas_call(kernel, out_shape=(jax.ShapeDtypeStruct(density.shape, bf1...  123 us
    unnamed x6, local copies, waits for them, and re-layouts  3.1 us

profile of v5, /device:TPU:88, one launch (start us, length us, event | category | flops | bytes accessed | tf_op | source)
XLA Modules:
  0.0 126.6 jit_solution(1435758023221975058)
XLA Ops:
  0.6 0.0 copy-start
  0.6 1.0 copy-done
  1.7 0.0 copy-start.1
  1.7 0.8 copy-done.1
  2.4 122.9 %shard_map.41 = (bf16[1024,256]{1,0:T(8,128)(2,1)S(1)}, f32[2]{0:T(128)S(1)}) custom-call(s32[64,64]{1,0:T(8,128)S(1)} %copy-done.1, bf16[1024,256]{1,0:T(8,128)(2,1)S(1)} %copy-done), custom_call_target="tpu_custom_call" | custom-call | flops 4294967296 | bytes 2097152 | tf_op jit(solution)/shard_map/pallas_call | solution.py:553
  125.3 0.8 copy.6
  126.1 0.5 copy.7
Async XLA Ops:
  0.6 1.0 copy-start
  1.7 0.8 copy-start.1

commit v6 on v5

--- a/solution.py
+++ b/solution.py
@@ -30,34 +30,34 @@
     (
         (
             (((), ()), ((), ())),
-            (((7, 6, 5,), (2, 3, 4,)), ((7, 6, 5, 4,), (2, 3,))),
-            (((7, 6, 5,), (3, 4,)), ((7, 6, 5,), (3, 4,))),
-            (((2, 7, 6,), (4, 5,)), ((0, 7, 6, 5,), (4,))),
-            (((), (1, 7, 6, 5,)), ((2, 7,), (5, 6,))),
+            (((7, 6, 5,), (2, 3, 4,)), ((7, 6, 5,), (2, 3, 4,))),
+            (((3, 4,), (7, 6, 5,)), ((3, 4, 5,), (7, 6,))),
+            (((4,), (1, 7, 6, 5,)), ((2, 7, 6,), (4, 5,))),
+            (((2, 7, 6, 5,), ()), ((5, 6,), (1, 7,))),
             (((), (2, 7, 6,)), ((6, 7,), ())),
-            (((), (3, 2, 7,)), ((7,), ())),
+            (((), (7,)), ((), (3, 0, 7,))),
             (((), ()), ((), ())),
         ),
     ),
     (
         (
             (((), ()), ((), ())),
-            (((6, 0,), ()), ((), (2, 0,))),
-            (((), (0, 7, 1,)), ((3, 1,), (6, 0,))),
-            (((4, 2, 0,), (1,)), ((1,), (4, 2, 0,))),
-            (((2, 3, 1,), (0,)), ((2, 0,), (5, 3, 1,))),
-            (((3, 1,), (4, 2, 0,)), ((2, 0, 4,), (3, 1,))),
-            (((7, 5, 3, 1,), (0, 2, 4,)), ((5, 3, 1,), (4, 2, 0,))),
+            (((), (4, 0,)), ((), (0,))),
+            (((), (3, 1, 0,)), ((0, 7, 1,), ())),
+            (((4, 2, 0,), (1,)), ((1,), (2, 0,))),
+            (((2, 0,), (3, 1,)), ((5, 3, 1,), (6, 0, 2,))),
+            (((4, 2, 0,), (3, 1,)), ((3, 1, 0,), (2, 4,))),
+            (((4, 2, 5,), (0, 3, 1,)), ((4, 2, 5,), (0, 1, 3,))),
             (((), ()), ((), ())),
         ),
         (
             (((), ()), ((), ())),
-            (((), (4, 0,)), ((0,), ())),
-            (((), (0, 1,)), ((5, 1, 0,), ())),
-            (((), (1, 0, 2,)), ((2, 0, 1,), ())),
-            (((0, 7, 1, 3,), (2,)), ((2, 6, 0,), (5, 3, 7, 1,))),
-            (((4, 2, 0,), (3, 1,)), ((3, 2, 4,), (1, 0,))),
-            (((4, 2,), (0, 1, 5, 3,)), ((0, 2, 4,), (7, 1, 3, 5,))),
+            (((6, 0,), ()), ((), (2, 0,))),
+            (((0, 7, 1,), ()), ((4, 6, 0,), (5, 3, 1,))),
+            (((5, 7, 1,), (4, 2, 0,)), ((1, 0, 2,), ())),
+            (((7, 1, 3,), (6, 0, 2,)), ((5, 3, 1,), (2, 0,))),
+            (((4, 2, 0,), (3, 1,)), ((2, 4,), (3, 1, 0,))),
+            (((4, 2, 5,), (0, 1, 3,)), ((1, 3, 5,), (4, 2, 0,))),
             (((), ()), ((), ())),
         ),
     ),
@@ -581,7 +581,7 @@
             dma((CHUNKS + 1,)), dma((CHUNKS + 1,)), dma((CHUNKS,)), dma((CHUNKS,)),
         ],
         compiler_params=pltpu.CompilerParams(
-            collective_id=0, has_side_effects=True, vmem_limit_bytes=40 * 1024 * 1024
+            collective_id=0, has_side_effects=True, vmem_limit_bytes=62 * 1024 * 1024
         ),
         cost_estimate=pl.CostEstimate(
             flops=2 * SUPER * SUPER * NSUP * TILE, bytes_accessed=2 * 1024 * 1024, transcendentals=0

time: 127 us -> 116 us (0.913)
  the two profiles are of different devices: /device:TPU:88 before, /device:TPU:218 now
where the time goes in v6:
time: 116 us
  Pallas kernels  113 us (97%)
  local copies, waits for them, and re-layouts  2.38 us (2%)
    pallas_call x1, Pallas kernels, per_device(): pl.pallas_call(kernel, out_shape=(jax.ShapeDtypeStruct(density.shape, bf1...  113 us
    unnamed x4, local copies, waits for them, and re-layouts  2.38 us

profile of v6, /device:TPU:218, one launch (start us, length us, event | category | flops | bytes accessed | tf_op | source)
XLA Modules:
  0.0 116.0 jit_solution(14962163028178141062)
XLA Ops:
  0.6 112.9 %shard_map.41 = (bf16[1024,256]{1,0:T(8,128)(2,1)}, f32[2]{0:T(128)}) custom-call(s32[64,64]{1,0:T(8,128)} %pat_in.1, bf16[1024,256]{1,0:T(8,128)(2,1)} %dens_in.1), custom_call_target="tpu_custom_call" | custom-call | flops 4294967296 | bytes 2097152 | tf_op jit(solution)/shard_map/pallas_call | solution.py:553
  113.6 0.0 copy-start
  113.6 1.9 %copy.6 = bf16[1024,256]{1,0:T(8,128)(2,1)} copy(bf16[1024,256]{1,0:T(8,128)(2,1)} %get-tuple-element.4) | data formatting | bytes 1048576
  115.4 0.0 copy-done
  115.4 0.5 copy.7
Async XLA Ops:
  113.6 1.9 %copy-start = (f32[2]{0:T(128)S(1)}, f32[2]{0:T(128)}, u32[]{:S(2)}) copy-start(f32[2]{0:T(128)} %get-tuple-element.5) | copy-start | bytes 28

commit v7 on v6

--- a/solution.py
+++ b/solution.py
@@ -64,6 +64,15 @@
 )
 
 
+def plain_order(p):
+    rows = []
+    for h in range(8):
+        hi = h // 4
+        xx = 7 - h if hi else h
+        rows.append(2 * ((xx + 2 * p) % 4) + hi)
+    return rows
+
+
 def chains(ring, p, center, parity):
     table, firsts = {}, []
     for places in CHAINS[ring][p][center][parity]:
@@ -84,6 +93,20 @@
         nexts.append(sum(table.get(i, (0, i))[1] * 8**i for i in range(8)))
         seconds.append(second)
     return depths, nexts, seconds
+
+
+def partners(ring, p):
+    order = plain_order(p) if ring else list(range(8))
+    masks = []
+    for center in range(8):
+        pairs = [(order[i], order[(i + 1) % 8]) for i in range(8)]
+        for parity in range(2):
+            table, second = chains(ring, p, center, parity)
+            pairs += [(i, following) for i, (_depth, following) in table.items()] + [(center, second)]
+        for me in range(8):
+            near = {b for a, b in pairs if a == me} | {a for a, b in pairs if b == me}
+            masks.append(sum(2**i for i in near - {me}))
+    return masks
 
 
 DEEPEST = max(
@@ -136,9 +159,21 @@
     others = [lax.rem(s + d, 4) for d in (1, 2, 3)]
 
     barrier = pltpu.get_barrier_semaphore()
-    for i in range(1, 8):
-        for device in (dev(r, wrap(z + i), s), dev(wrap(r + i), z, s)):
-            pl.semaphore_signal(barrier, inc=1, device_id=device, device_id_type=MESH)
+    greeted = jnp.int32(3)
+    masks = (
+        pick(partners(0, 0), r * 8 + z),
+        jnp.where(p == 0, pick(partners(1, 0), z * 8 + r), pick(partners(1, 1), z * 8 + r)),
+    )
+    for ring in range(2):
+        for i in range(8):
+            near = lax.rem(lax.div(masks[ring], 2**i), 2)
+            greeted = greeted + near
+
+            @pl.when(near == 1)
+            def _():
+                device = dev(r, i, s) if ring == 0 else dev(i, z, s)
+                pl.semaphore_signal(barrier, inc=1, device_id=device, device_id_type=MESH)
+
     for o in others:
         pl.semaphore_signal(barrier, inc=1, device_id=dev(r, z, o), device_id_type=MESH)
 
@@ -174,7 +209,7 @@
     tr[0, z, 0:8, :] = first.reshape(BLK // 8, 8, BLK).sum(axis=0)
     tr[0, z, 8:16, :] = second.reshape(BLK // 8, 8, BLK).sum(axis=0)
 
-    pl.semaphore_wait(barrier, 17)
+    pl.semaphore_wait(barrier, greeted)
 
     def intra(o):
         return copy(

time: 116 us -> 115 us (level)
  no operation moved by 1% of the time
where the time goes in v7:
time: 115 us
  Pallas kernels  112 us (97%)
  local copies, waits for them, and re-layouts  2.38 us (2%)
    pallas_call x1, Pallas kernels, per_device(): pl.pallas_call(kernel, out_shape=(jax.ShapeDtypeStruct(density.shape, bf1...  112 us
    unnamed x4, local copies, waits for them, and re-layouts  2.38 us

profile of v7, /device:TPU:218, one launch (start us, length us, event | category | flops | bytes accessed | tf_op | source)
XLA Modules:
  0.0 114.8 jit_solution(11648287962926326759)
XLA Ops:
  0.6 111.8 %shard_map.41 = (bf16[1024,256]{1,0:T(8,128)(2,1)}, f32[2]{0:T(128)}) custom-call(s32[64,64]{1,0:T(8,128)} %pat_in.1, bf16[1024,256]{1,0:T(8,128)(2,1)} %dens_in.1), custom_call_target="tpu_custom_call" | custom-call | flops 4294967296 | bytes 2097152 | tf_op jit(solution)/shard_map/pallas_call | solution.py:588
  112.5 0.0 copy-start
  112.5 1.9 %copy.6 = bf16[1024,256]{1,0:T(8,128)(2,1)} copy(bf16[1024,256]{1,0:T(8,128)(2,1)} %get-tuple-element.4) | data formatting | bytes 1048576
  114.3 0.0 copy-done
  114.3 0.5 copy.7
Async XLA Ops:
  112.5 1.9 %copy-start = (f32[2]{0:T(128)S(1)}, f32[2]{0:T(128)}, u32[]{:S(2)}) copy-start(f32[2]{0:T(128)} %get-tuple-element.5) | copy-start | bytes 28
